TPU v7x, 512 devices: a whole 4x4x16 slice. The times are simulated.
512 devices in a mesh: space: 32 (over z, core), tm: 16 (over x, y).
Axes of the slice: x: 4, y: 4, z: 16, core: 2. Of those that a mesh axis runs over, the one named last changes fastest.
Arguments:
- recordings: bfloat16 [2, 3, 512, 32768], P(None, None, 'space', 'tm'), may hold values from -30 to 30
- owner: int32 [512, 1], P('space'), may hold values from 0 to 31; in each aligned block of 16 rows (0 to 15, 16 to 31, ...) at most 2 rows name the same one
- valid_range: int32 [512, 2], P('space'), may hold values from 0 to 32768, as said below
- bin_mask: int32 [512, 96], P('space'), may hold values 0 or 1
Outputs:
- adjoint: bfloat16 [3, 2048, 32768], P(None, 'space', 'tm')
Inputs may be any that keep to these rules, and one draw needn't show every extreme that they name: `owner`: among the 16 receivers listed on one index of space, no subdomain owns more than 2; some subdomain owns exactly 2 of them. `valid_range`: column 0 is below column 1 in every row.
All inputs are finite; a program needn't handle non-finite values. No bound on the sum of `bin_mask` on one device may be relied on, other than what follows from the above.
Results may differ from a plain program's by a relative error of at most 0.013.
Values may be sent and summed in bfloat16 or wider, within the bound.
A program may use at most 128 MiB of HBM per device.

v0:
```python
import math
import jax
import jax.numpy as jnp
from jax import lax
from jax.sharding import PartitionSpec as P

BINS = 96
HOP = 256
HALO = 1024
KERNEL = 2304
WATER = 0.1
EPSILON = 1e-06


def with_halo(block, sides, width):
    for axis, dim in sides:
        count = lax.axis_size(axis)
        forward = [(i, i + 1) for i in range(count - 1)]
        backward = [(target, source) for source, target in forward]
        low = lax.ppermute(
            lax.slice_in_dim(block, block.shape[dim] - width, None, axis=dim), axis, forward
        )
        high = lax.ppermute(lax.slice_in_dim(block, 0, width, axis=dim), axis, backward)
        block = jnp.concatenate([low, block, high], axis=dim)
    return block


def shifted(block, axis, distance):
    devices = range(lax.axis_size(axis))
    route = [(i - distance, i) for i in devices if i - distance in devices]
    return lax.ppermute(block, axis, route)


def cq_kernel(kern_len, bins):
    octave_bins = bins // 8
    index = jnp.arange(bins).astype(jnp.float32)
    freq = 0.25 * jnp.exp2((index - (bins - 1)) / octave_bins)
    quality = 1.0 / (2.0 ** (1.0 / octave_bins) - 1.0)
    support = jnp.minimum(quality / freq, float(kern_len))
    offset = jnp.arange(kern_len).astype(jnp.float32) - 0.5 * (kern_len - 1)
    ratio = offset[:, None] / support[None, :]
    window = jnp.where(jnp.abs(ratio) < 0.5, 0.5 + 0.5 * jnp.cos(2.0 * math.pi * ratio), 0.0)
    window = window / jnp.sqrt(jnp.sum(window * window, axis=0, keepdims=True))
    cycles = offset[:, None] * freq[None, :]
    phase = cycles - jnp.floor(cycles)
    table = jnp.concatenate(
        [window * jnp.cos(2.0 * math.pi * phase), -window * jnp.sin(2.0 * math.pi * phase)], axis=1
    )
    return table.astype(jnp.bfloat16)


def adjoint_of(syn_re, syn_im, obs_re, obs_im, weight):
    level = (
        WATER * jnp.mean(obs_re * obs_re + obs_im * obs_im, axis=(-2, -1), keepdims=True) + EPSILON
    )
    syn_norm = jnp.sqrt(syn_re * syn_re + syn_im * syn_im + level)
    obs_norm = jnp.sqrt(obs_re * obs_re + obs_im * obs_im + level)
    diff_re = weight * (syn_re / syn_norm - obs_re / obs_norm)
    diff_im = weight * (syn_im / syn_norm - obs_im / obs_norm)
    inner = (syn_re * diff_re + syn_im * diff_im) / (syn_norm * syn_norm * syn_norm)
    return (diff_re / syn_norm - syn_re * inner, diff_im / syn_norm - syn_im * inner)


def analyse(blocks, table, frames):
    taps = table.shape[0] // HOP
    unfolded = jnp.concatenate([blocks[..., tap : tap + frames, :] for tap in range(taps)], axis=-1)
    return jnp.einsum("...fh,hk->...fk", unfolded, table, preferred_element_type=jnp.float32)


def synthesise(coefs, table, frames):
    taps = table.shape[0] // HOP
    term = jnp.einsum("...fk,hk->...fh", coefs, table, preferred_element_type=jnp.float32)
    term = term.reshape(term.shape[:-1] + (taps, HOP))
    lead = len(term.shape) - 3
    ext = jnp.zeros(coefs.shape[:-2] + (frames + taps - 1, HOP), jnp.float32)
    for tap in range(taps):
        widths = [(0, 0)] * lead + [(tap, taps - 1 - tap), (0, 0)]
        ext = ext + jnp.pad(term[..., tap, :], widths)
    return ext


def frame_weight(ranges, masks, frames_all):
    centers = jnp.arange(frames_all, dtype=jnp.int32) * HOP + HOP // 2
    inside = (ranges[:, 0:1] <= centers[None, :]) & (centers[None, :] < ranges[:, 1:2])
    return inside.astype(jnp.float32)[:, :, None] * masks.astype(jnp.float32)[:, None, :]


def misfit(coefs, weight):
    adj_re, adj_im = adjoint_of(
        coefs[0, ..., :BINS],
        coefs[0, ..., BINS:],
        coefs[1, ..., :BINS],
        coefs[1, ..., BINS:],
        weight,
    )
    joined = jnp.concatenate([adj_re, adj_im], axis=-1)
    return joined.reshape(joined.shape[:2] + (joined.shape[2] * joined.shape[3],)).astype(
        jnp.bfloat16
    )


def on_device(recordings, owner, valid_range, bin_mask):
    table = cq_kernel(KERNEL, BINS)
    margin = HALO // HOP
    width = 2 * BINS
    groups = lax.axis_size("tm")
    comps = recordings.shape[1]
    rec_dev = recordings.shape[2]
    samples_dev = recordings.shape[3]
    frames_dev = samples_dev // HOP
    rec_group = rec_dev // groups
    first_row = lax.axis_index("tm") * rec_group
    ranges = lax.dynamic_slice_in_dim(valid_range, first_row, rec_group, 0)
    masks = lax.dynamic_slice_in_dim(bin_mask, first_row, rec_group, 0)
    extended = with_halo(recordings, (("tm", 3),), HALO)
    blocks = extended.reshape(2, comps, rec_dev, frames_dev + 2 * margin, HOP)
    coefs = analyse(blocks, table, frames_dev)
    packed = coefs.astype(jnp.bfloat16).reshape(2, comps, rec_dev, frames_dev * width)
    weight = frame_weight(ranges, masks, frames_dev * groups)
    pieces = lax.all_to_all(packed, "tm", split_axis=2, concat_axis=3, tiled=True)
    items = pieces.shape[1]
    frames_all = pieces.shape[3] // width
    local_coefs = pieces.astype(jnp.float32).reshape(2, items, rec_group, frames_all, width)
    adjoint_local = misfit(local_coefs, weight)
    adjoint_back = lax.all_to_all(adjoint_local, "tm", split_axis=2, concat_axis=1, tiled=True)
    adjoint_frames = adjoint_back.reshape(comps, rec_dev, frames_dev, width)
    ext = synthesise(adjoint_frames, table, frames_dev)
    flat = ext.reshape(comps, rec_dev, (frames_dev + 2 * margin) * HOP)
    middle = flat[:, :, HALO : HALO + samples_dev]
    from_before = shifted(flat[:, :, HALO + samples_dev :].astype(jnp.bfloat16), "tm", 1).astype(
        jnp.float32
    )
    from_after = shifted(flat[:, :, :HALO].astype(jnp.bfloat16), "tm", -1).astype(jnp.float32)
    middle = middle.at[:, :, :HALO].add(from_before)
    middle = middle.at[:, :, samples_dev - HALO :].add(from_after)
    series = middle.astype(jnp.bfloat16)
    count = lax.axis_size("space")
    most = max(2, 3 * rec_dev // (2 * count))
    target = owner[:, 0]
    place = jnp.arange(rec_dev, dtype=jnp.int32)
    earlier = (target[:, None] == target[None, :]) & (place[None, :] < place[:, None])
    rank = jnp.sum(earlier.astype(jnp.int32), axis=1)
    slot = target * most + rank
    select = (jnp.arange(count * most, dtype=jnp.int32)[:, None] == slot[None, :]).astype(
        jnp.bfloat16
    )
    outgoing = jnp.einsum("sr,crt->cst", select, series, preferred_element_type=jnp.float32).astype(
        jnp.bfloat16
    )
    return lax.all_to_all(outgoing, "space", split_axis=1, concat_axis=1, tiled=True)


def solution(mesh):
    return jax.shard_map(
        on_device,
        mesh=mesh,
        in_specs=(
            P(None, None, "space", "tm"),
            P("space", None),
            P("space", None),
            P("space", None),
        ),
        out_specs=P(None, "space", "tm"),
        check_vma=False,
    )
```

profile of v0, /device:TPU:25, one launch (start us, length us, event | category | flops | bytes accessed | tf_op | source)
XLA Modules:
  0.0 341.8 jit_solution(2724905111548227926)
XLA Ops:
  0.0 0.0 copy-start
  0.0 1.1 fusion.24
  1.1 2.8 collective-permute-start
  3.9 2.5 collective-permute-start.1
  6.4 3.4 %multiply_reduce_fusion = f32[96]{0:T(128)S(1)} fusion(f32[96]{0:T(128)S(1)} %get-tuple-element.50, f32[2304]{0:T(1024)S(1)} %convert_add_fusion.1), kind=kLoop, calls=%fused_computation.20 | loop fusion | flops 1990560 | bytes 9984 | tf_op jit(solution)/shard_map/reduce_sum | solution.py:43
  9.9 0.0 copy-done
  9.9 0.1 constant_dynamic-slice_fusion.1
  9.9 0.6 fusion.25
  10.5 6.6 %multiply_convert_fusion.3 = (bf16[2304,96]{0,1:T(8,128)(2,1)S(1)}, bf16[2304,96]{0,1:T(8,128)(2,1)S(1)}) fusion(f32[96]{0:T(128)S(1)} %get-tuple-element.51, f32[2304]{0:T(1024)S(1)} %convert_add_fusion.1, f32[96]{0:T(128)S(1)} %sqrt.38, f32[96]{0:T(128)S(1)} %get-tuple-element.50), kind=kLoop, calls=%fused_computation.19 | loop fusion | flops 3760128 | bytes 895104 | tf_op jit(solution)/shard_map/convert.7
  17.2 0.7 fusion.19
  17.9 0.0 collective-permute-done
  17.9 0.0 collective-permute-done.1
  17.9 1.1 pad_maximum_fusion
  19.0 0.2 copy.106
  19.2 0.1 slice_dynamic-update-slice_fusion.7
  19.3 0.1 slice_dynamic-update-slice_fusion.6
  19.4 0.1 slice_dynamic-update-slice_fusion.5
  19.6 0.1 slice_dynamic-update-slice_fusion.4
  19.7 0.1 slice_dynamic-update-slice_fusion.3
  19.8 0.1 slice_dynamic-update-slice_fusion.2
  19.9 0.1 slice_dynamic-update-slice_fusion.1
  20.1 1.1 convolution_convert_fusion.1
  21.2 0.3 reshape.521
  21.6 1.0 copy.78
  22.6 6.6 %all-to-all-start = ((bf16[2,3,16,1536]{3,0,1,2:T(2,128)(2,1)}), bf16[2,3,16,1536]{3,0,1,2:T(2,128)(2,1)S(1)}, u32[]{:S(2)}, u32[]{:S(2)}) async-start(bf16[2,3,16,1536]{3,0,1,2:T(2,128)(2,1)} %copy.78), calls=%async_computation | async-start | bytes 589824 | tf_op jit(solution)/shard_map/all_to_all | solution.py:120
  29.2 1.3 and_convert_fusion
  30.4 0.1 broadcast_multiply_fusion
  30.5 4.4 %all-to-all-done = bf16[2,3,16,1536]{3,0,1,2:T(2,128)(2,1)S(1)} async-done(((bf16[2,3,16,1536]{3,0,1,2:T(2,128)(2,1)}), bf16[2,3,16,1536]{3,0,1,2:T(2,128)(2,1)S(1)}, u32[]{:S(2)}, u32[]{:S(2)}) %all-to-all-start) | async-done | bytes 294944 | tf_op jit(solution)/shard_map/all_to_all | solution.py:120
  34.9 0.1 copy_convert_fusion
  34.9 0.2 reshape.524
  35.2 0.2 fusion.22
  35.4 0.4 subtract_convert_fusion.1
  35.8 0.1 pad_maximum_fusion.1
  35.9 0.2 convert_element_type.135
  36.2 19.4 %copy.83 = bf16[3,1,24576]{0,1,2:T(2,128)(2,1)} copy(bf16[3,1,24576]{2,0,1:T(4,128)(2,1)S(1)} %convert_element_type.135) | data formatting | bytes 294912 | tf_op jit(solution)/shard_map/convert_element_type | solution.py:97
  55.6 0.5 broadcast.336
  56.1 135.0 %reduce.5 = bf16[24576,3]{1,0:T(8,128)(2,1)} reduce(bf16[24576,1,3]{2,1,0:T(2,128)(2,1)} %bitcast.152, bf16[]{:T(256)} %broadcast.336), dimensions={1}, to_apply=%bitcast.148.reduce_sub_computation | reduce | bytes 294914
  191.1 0.0 copy-start.1
  191.1 10.0 %reshape.530 = bf16[16,2,2304]{2,1,0:T(2,128)(2,1)} reshape(bf16[24576,3]{1,0:T(8,128)(2,1)} %reduce.5) | data formatting | bytes 294912
  201.1 5.5 %all-to-all-start.1 = ((bf16[16,2,2304]{2,1,0:T(2,128)(2,1)}), bf16[16,2,2304]{2,1,0:T(2,128)(2,1)S(1)}, u32[]{:S(2)}, u32[]{:S(2)}) async-start(bf16[16,2,2304]{2,1,0:T(2,128)(2,1)} %reshape.530), calls=%async_computation.1 | async-start | bytes 294912 | tf_op jit(solution)/shard_map/all_to_all | solution.py:125
  206.5 6.8 %multiply_convert_fusion.1 = (bf16[9,256,96]{1,2,0:T(8,128)(2,1)S(1)}, bf16[9,256,96]{1,2,0:T(8,128)(2,1)S(1)}) fusion(f32[96]{0:T(128)S(1)} %get-tuple-element.51, f32[9,256]{1,0:T(8,128)S(1)} %convert_add_fusion, f32[96]{0:T(128)S(1)} %sqrt.38, f32[96]{0:T(128)S(1)} %get-tuple-element.50), kind=kLoop, calls=%fused_computation.15 | loop fusion | flops 3760128 | bytes 895104 | tf_op jit(solution)/shard_map/convert.3
  213.4 0.0 copy-done.1
  213.4 0.2 convert_reduce_fusion
  213.6 0.0 all-to-all-done.1
  213.6 14.5 %reshape.531 = bf16[24576,1,3]{2,1,0:T(2,128)(2,1)} reshape(bf16[16,2,2304]{2,1,0:T(2,128)(2,1)S(1)} %all-to-all-done.1) | data formatting | bytes 294912
  228.0 23.3 %copy.84 = bf16[3,1,24576]{2,0,1:T(4,128)(2,1)S(1)} copy(bf16[3,1,24576]{0,1,2:T(2,128)(2,1)} %bitcast.151) | data formatting | bytes 294912 | tf_op jit(solution)/shard_map/all_to_all | solution.py:125
  251.4 0.2 reshape.526
  251.6 0.6 fusion.5
  252.2 0.4 slice_bitcast_fusion.8
  252.7 0.5 pad_add_fusion
  253.2 0.1 reshape.523
  253.4 3.1 collective-permute-start.2
  256.6 2.2 collective-permute-start.3
  258.8 0.0 collective-permute-done.2
  258.8 5.2 %collective-permute-done.3 = bf16[3,16,1024]{2,1,0:T(8,128)(2,1)S(1)} collective-permute-done((bf16[3,16,1024]{2,1,0:T(8,128)(2,1)S(1)}, bf16[3,16,1024]{2,1,0:T(8,128)(2,1)S(1)}, u32[]{:S(2)}, u32[]{:S(2)}) %collective-permute-start.3) | collective-permute-done | bytes 98336 | tf_op jit(solution)/shard_map/ppermute | solution.py:31
  264.1 0.5 fusion
  264.6 0.7 copy.93
  265.3 75.1 %all_to_all.23 = bf16[3,64,2048]{2,0,1:T(4,128)(2,1)S(1)} all-to-all(bf16[3,64,2048]{2,0,1:T(4,128)(2,1)S(1)} %copy.93), channel_id=1, replica_groups=mesh['space'=32,'tm'=16] {'space'}, dimensions={1} | all-to-all | bytes 1572864 | tf_op jit(solution)/shard_map/all_to_all | solution.py:150
  340.4 1.5 copy.94
  (13 shorter events, 0.2 us)
Async XLA Ops:
  0.0 9.9 %copy-start = (s32[16,2]{0,1:T(2,128)S(1)}, s32[16,2]{0,1:T(2,128)}, u32[]{:S(2)}) copy-start(s32[16,2]{0,1:T(2,128)} %param.10) | copy-start | bytes 388
  1.1 16.8 %collective-permute-start = (bf16[2,3,16,1024]{3,2,1,0:T(8,128)(2,1)S(1)}, bf16[2,3,16,1024]{3,2,1,0:T(8,128)(2,1)S(1)}, u32[]{:S(2)}, u32[]{:S(2)}) collective-permute-start(bf16[2,3,16,1024]{3,2,1,0:T(8,128)(2,1)S(1)} %get-tuple-element.42), channel_id=1, source_target_pairs={{0,1},{1,2},{2,3},{3,4},{4,5},{5,6},{6,7},{7,8},{8,9},{9,10},{10,1... | collective-permute-start | bytes 589832 | tf_op jit(solution)/shard_map/ppermute | solution.py:20
  3.9 14.1 %collective-permute-start.1 = (bf16[2,3,16,1024]{3,2,1,0:T(8,128)(2,1)S(1)}, bf16[2,3,16,1024]{3,2,1,0:T(8,128)(2,1)S(1)}, u32[]{:S(2)}, u32[]{:S(2)}) collective-permute-start(bf16[2,3,16,1024]{3,2,1,0:T(8,128)(2,1)S(1)} %get-tuple-element.43), channel_id=1, source_target_pairs={{1,0},{2,1},{3,2},{4,3},{5,4},{6,5},{7,6},{8,7},{9,8},{10,9},{11,1... | collective-permute-start | bytes 589832 | tf_op jit(solution)/shard_map/ppermute | solution.py:23
  22.6 12.3 %all-to-all-start = ((bf16[2,3,16,1536]{3,0,1,2:T(2,128)(2,1)}), bf16[2,3,16,1536]{3,0,1,2:T(2,128)(2,1)S(1)}, u32[]{:S(2)}, u32[]{:S(2)}) async-start(bf16[2,3,16,1536]{3,0,1,2:T(2,128)(2,1)} %copy.78), calls=%async_computation | async-start | bytes 589824 | tf_op jit(solution)/shard_map/all_to_all | solution.py:120
  191.1 22.3 %copy-start.1 = (s32[16,1]{0,1:T(1,128)S(1)}, s32[16,1]{0,1:T(1,128)}, u32[]{:S(2)}) copy-start(s32[16,1]{0,1:T(1,128)} %param.9) | copy-start | bytes 196
  201.1 12.5 %all-to-all-start.1 = ((bf16[16,2,2304]{2,1,0:T(2,128)(2,1)}), bf16[16,2,2304]{2,1,0:T(2,128)(2,1)S(1)}, u32[]{:S(2)}, u32[]{:S(2)}) async-start(bf16[16,2,2304]{2,1,0:T(2,128)(2,1)} %reshape.530), calls=%async_computation.1 | async-start | bytes 294912 | tf_op jit(solution)/shard_map/all_to_all | solution.py:125
  253.4 5.4 %collective-permute-start.2 = (bf16[3,16,1024]{2,1,0:T(8,128)(2,1)S(1)}, bf16[3,16,1024]{2,1,0:T(8,128)(2,1)S(1)}, u32[]{:S(2)}, u32[]{:S(2)}) collective-permute-start(bf16[3,16,1024]{2,1,0:T(8,128)(2,1)S(1)} %get-tuple-element.41), channel_id=1, source_target_pairs={{0,1},{1,2},{2,3},{3,4},{4,5},{5,6},{6,7},{7,8},{8,9},{9,10},{10,1... | collective-permute-start | bytes 294920 | tf_op jit(solution)/shard_map/ppermute | solution.py:31
  256.6 7.5 %collective-permute-start.3 = (bf16[3,16,1024]{2,1,0:T(8,128)(2,1)S(1)}, bf16[3,16,1024]{2,1,0:T(8,128)(2,1)S(1)}, u32[]{:S(2)}, u32[]{:S(2)}) collective-permute-start(bf16[3,16,1024]{2,1,0:T(8,128)(2,1)S(1)} %get-tuple-element.40), channel_id=1, source_target_pairs={{1,0},{2,1},{3,2},{4,3},{5,4},{6,5},{7,6},{8,7},{9,8},{10,9},{11,1... | collective-permute-start | bytes 294920 | tf_op jit(solution)/shard_map/ppermute | solution.py:31
where the time goes:
time: 343 us; the launch traced here: 342 us
  other arithmetic  157 us (46%)
  local copies, waits for them, and re-layouts  75.3 us (22%)
  blocking collectives  75.1 us (22%)
  starting transfers between devices  22.7 us (7%)
  waiting for transfers between devices  9.61 us (3%)
    unnamed x1, other arithmetic  135 us
    all_to_all x1, blocking collectives, on_device(): lax.all_to_all(outgoing, 'space', split_axis=1, concat_axis=1, tiled=True)  75.1 us
    unnamed x16, local copies, waits for them, and re-layouts  26 us
    all_to_all x1, local copies, waits for them, and re-layouts, on_device(): lax.all_to_all(adjoint_local, 'tm', split_axis=2, concat_axis=1, tiled=True)  23.3 us
    convert_element_type x2, local copies, waits for them, and re-layouts, misfit(): joined.reshape(joined.shape[:2] + (joined.shape[2] * joined.shape[3],))  19.7 us
    another operation x4, other arithmetic  13.9 us
  transfers between devices with their start and end apart: 6, of which 2 were waited for; matrix products, arithmetic and copies ran while one was open for 6% of the time, Pallas kernels for 0%

commit v1 on v0

--- a/solution.py
+++ b/solution.py
@@ -122,7 +122,12 @@
     frames_all = pieces.shape[3] // width
     local_coefs = pieces.astype(jnp.float32).reshape(2, items, rec_group, frames_all, width)
     adjoint_local = misfit(local_coefs, weight)
-    adjoint_back = lax.all_to_all(adjoint_local, "tm", split_axis=2, concat_axis=1, tiled=True)
+    adjoint_back = jnp.concatenate(
+        lax.all_to_all(
+            jnp.stack(jnp.split(adjoint_local, lax.axis_size("tm"), axis=2)), "tm", 0, 0
+        ),
+        axis=1,
+    )
     adjoint_frames = adjoint_back.reshape(comps, rec_dev, frames_dev, width)
     ext = synthesise(adjoint_frames, table, frames_dev)
     flat = ext.reshape(comps, rec_dev, (frames_dev + 2 * margin) * HOP)

time: 343 us -> 149 us (0.43)
  other arithmetic: 157 us -> 21.6 us
  local copies, waits for them, and re-layouts: 75.3 us -> 17.2 us
    unnamed x1 -> x0, other arithmetic: 135 us -> none
    all_to_all x1 -> x0, local copies, waits for them, and re-layouts: 23.3 us -> none  [on_device(): lax.all_to_all(adjoint_local, 'tm', split_axis=2, concat_axis=1, tiled=True)]
    convert_element_type x2 -> x1, local copies, waits for them, and re-layouts: 19.7 us -> 0.25 us  [misfit(): joined.reshape(joined.shape[:2] + (joined.shape[2] * joined.shape[3],))]
    unnamed x16 -> x28, local copies, waits for them, and re-layouts: 26 us -> 10.1 us
  transfers between devices with their start and end apart: 6 -> 6, of which waited for: 2 -> 2; matrix products, arithmetic and copies ran while one was open for 6% -> 13% of each run, Pallas kernels for 0% -> 0%
where the time goes in v1:
time: 149 us
  blocking collectives  75.1 us (50%)
  starting transfers between devices  22.8 us (15%)
  other arithmetic  21.6 us (14%)
  local copies, waits for them, and re-layouts  17.2 us (12%)
  waiting for transfers between devices  9.59 us (6%)
  matrix products  2.21 us (1%)
    all_to_all x1, blocking collectives, on_device(): lax.all_to_all(outgoing, 'space', split_axis=1, concat_axis=1, tiled=True)  75.1 us
    another operation x4, other arithmetic  13.9 us
    unnamed x28, local copies, waits for them, and re-layouts  10.1 us
    all_to_all x1, starting transfers between devices, on_device(): lax.all_to_all(packed, 'tm', split_axis=2, concat_axis=3, tiled=True)  6.74 us
    all_to_all x1, starting transfers between devices, on_device(): lax.all_to_all(jnp.stack(jnp.split(adjoint_local, lax.axis_size('tm'), ax...  5.5 us
    ppermute x2, starting transfers between devices, shifted(): return lax.ppermute(block, axis, route)  5.28 us
    ppermute x2, waiting for transfers between devices, shifted(): return lax.ppermute(block, axis, route)  5.25 us
    all_to_all x1, waiting for transfers between devices, on_device(): lax.all_to_all(packed, 'tm', split_axis=2, concat_axis=3, tiled=True)  4.34 us
  transfers between devices with their start and end apart: 6, of which 2 were waited for; matrix products, arithmetic and copies ran while one was open for 13% of the time, Pallas kernels for 0%

profile of v1, /device:TPU:25, one launch (start us, length us, event | category | flops | bytes accessed | tf_op | source)
XLA Modules:
  0.0 149.0 jit_solution(8929880964629543283)
XLA Ops:
  0.0 1.1 fusion.24
  1.1 2.8 %collective-permute-start = (bf16[2,3,16,1024]{3,2,1,0:T(8,128)(2,1)S(1)}, bf16[2,3,16,1024]{3,2,1,0:T(8,128)(2,1)S(1)}, u32[]{:S(2)}, u32[]{:S(2)}) collective-permute-start(bf16[2,3,16,1024]{3,2,1,0:T(8,128)(2,1)S(1)} %get-tuple-element.42), channel_id=1, source_target_pairs={{0,1},{1,2},{2,3},{3,4},{4,5},{5,6},{6,7},{7,8},{8,9},{9,10},{10,1... | collective-permute-start | bytes 589832 | tf_op jit(solution)/shard_map/ppermute | solution.py:20
  3.9 2.5 %collective-permute-start.1 = (bf16[2,3,16,1024]{3,2,1,0:T(8,128)(2,1)S(1)}, bf16[2,3,16,1024]{3,2,1,0:T(8,128)(2,1)S(1)}, u32[]{:S(2)}, u32[]{:S(2)}) collective-permute-start(bf16[2,3,16,1024]{3,2,1,0:T(8,128)(2,1)S(1)} %get-tuple-element.43), channel_id=1, source_target_pairs={{1,0},{2,1},{3,2},{4,3},{5,4},{6,5},{7,6},{8,7},{9,8},{10,9},{11,1... | collective-permute-start | bytes 589832 | tf_op jit(solution)/shard_map/ppermute | solution.py:23
  6.4 3.4 %multiply_reduce_fusion = f32[96]{0:T(128)S(1)} fusion(f32[96]{0:T(128)S(1)} %get-tuple-element.50, f32[2304]{0:T(1024)S(1)} %convert_add_fusion.1), kind=kLoop, calls=%fused_computation.20 | loop fusion | flops 1990560 | bytes 9984 | tf_op jit(solution)/shard_map/reduce_sum | solution.py:43
  9.9 0.1 constant_dynamic-slice_fusion.1
  9.9 0.6 fusion.25
  10.5 6.6 %multiply_convert_fusion.3 = (bf16[2304,96]{0,1:T(8,128)(2,1)S(1)}, bf16[2304,96]{0,1:T(8,128)(2,1)S(1)}) fusion(f32[96]{0:T(128)S(1)} %get-tuple-element.51, f32[2304]{0:T(1024)S(1)} %convert_add_fusion.1, f32[96]{0:T(128)S(1)} %sqrt.38, f32[96]{0:T(128)S(1)} %get-tuple-element.50), kind=kLoop, calls=%fused_computation.19 | loop fusion | flops 3760128 | bytes 895104 | tf_op jit(solution)/shard_map/convert.7
  17.2 0.7 fusion.19
  17.9 0.0 collective-permute-done
  17.9 0.0 collective-permute-done.1
  17.9 1.1 pad_maximum_fusion
  18.9 0.2 copy.118
  19.2 0.1 slice_dynamic-update-slice_fusion.7
  19.3 0.1 slice_dynamic-update-slice_fusion.6
  19.4 0.1 slice_dynamic-update-slice_fusion.5
  19.5 0.1 slice_dynamic-update-slice_fusion.4
  19.7 0.1 slice_dynamic-update-slice_fusion.3
  19.8 0.1 slice_dynamic-update-slice_fusion.2
  19.9 0.1 slice_dynamic-update-slice_fusion.1
  20.1 1.1 convolution_convert_fusion.1
  21.2 0.3 reshape.517
  21.5 1.0 copy.91
  22.5 6.7 %all-to-all-start = ((bf16[2,3,16,1536]{3,0,1,2:T(2,128)(2,1)}), bf16[2,3,16,1536]{3,0,1,2:T(2,128)(2,1)S(1)}, u32[]{:S(2)}, u32[]{:S(2)}) async-start(bf16[2,3,16,1536]{3,0,1,2:T(2,128)(2,1)} %copy.91), calls=%async_computation | async-start | bytes 589824 | tf_op jit(solution)/shard_map/all_to_all | solution.py:120
  29.3 1.3 and_convert_fusion
  30.5 0.1 broadcast_multiply_fusion
  30.6 4.3 %all-to-all-done = bf16[2,3,16,1536]{3,0,1,2:T(2,128)(2,1)S(1)} async-done(((bf16[2,3,16,1536]{3,0,1,2:T(2,128)(2,1)}), bf16[2,3,16,1536]{3,0,1,2:T(2,128)(2,1)S(1)}, u32[]{:S(2)}, u32[]{:S(2)}) %all-to-all-start) | async-done | bytes 294944 | tf_op jit(solution)/shard_map/all_to_all | solution.py:120
  35.0 0.1 copy_convert_fusion
  35.0 0.2 reshape.520
  35.3 0.2 fusion.22
  35.5 0.4 subtract_convert_fusion.1
  35.9 0.1 pad_maximum_fusion.1
  36.0 0.2 convert_element_type.135
  36.3 0.6 constant_dynamic-update-slice_fusion.15
  36.9 0.6 constant_dynamic-update-slice_fusion.14
  37.5 0.6 constant_dynamic-update-slice_fusion.13
  38.1 0.6 constant_dynamic-update-slice_fusion.12
  38.7 0.6 constant_dynamic-update-slice_fusion.11
  39.3 0.6 constant_dynamic-update-slice_fusion.10
  39.9 0.6 constant_dynamic-update-slice_fusion.9
  40.5 0.6 constant_dynamic-update-slice_fusion.8
  41.1 0.6 constant_dynamic-update-slice_fusion.7
  41.7 0.6 constant_dynamic-update-slice_fusion.6
  42.3 0.6 constant_dynamic-update-slice_fusion.5
  42.9 0.6 constant_dynamic-update-slice_fusion.4
  43.5 0.6 constant_dynamic-update-slice_fusion.3
  44.1 0.6 constant_dynamic-update-slice_fusion.2
  44.7 0.6 constant_dynamic-update-slice_fusion.1
  45.3 0.6 constant_dynamic-update-slice_fusion
  46.0 5.5 %all-to-all-start.1 = ((bf16[16,3,1,1536]{3,1,2,0:T(4,128)(2,1)}), bf16[16,3,1,1536]{3,1,2,0:T(4,128)(2,1)S(1)}, u32[]{:S(2)}, u32[]{:S(2)}) async-start(bf16[16,3,1,1536]{3,1,2,0:T(4,128)(2,1)} %constant_dynamic-update-slice_fusion), calls=%async_computation.1 | async-start | bytes 393216 | tf_op jit(solution)/shard_map/all_to_all | solution.py:126
  51.5 6.8 %multiply_convert_fusion.1 = (bf16[9,256,96]{1,2,0:T(8,128)(2,1)S(1)}, bf16[9,256,96]{1,2,0:T(8,128)(2,1)S(1)}) fusion(f32[96]{0:T(128)S(1)} %get-tuple-element.51, f32[9,256]{1,0:T(8,128)S(1)} %convert_add_fusion, f32[96]{0:T(128)S(1)} %sqrt.38, f32[96]{0:T(128)S(1)} %get-tuple-element.50), kind=kLoop, calls=%fused_computation.15 | loop fusion | flops 3760128 | bytes 895104 | tf_op jit(solution)/shard_map/convert.3
  58.3 0.2 convert_reduce_fusion
  58.5 0.2 reshape.522
  58.7 0.6 fusion.5
  59.3 0.4 slice_bitcast_fusion.8
  59.8 0.5 pad_add_fusion
  60.3 0.1 reshape.519
  60.6 3.1 %collective-permute-start.2 = (bf16[3,16,1024]{2,1,0:T(8,128)(2,1)S(1)}, bf16[3,16,1024]{2,1,0:T(8,128)(2,1)S(1)}, u32[]{:S(2)}, u32[]{:S(2)}) collective-permute-start(bf16[3,16,1024]{2,1,0:T(8,128)(2,1)S(1)} %get-tuple-element.41), channel_id=1, source_target_pairs={{0,1},{1,2},{2,3},{3,4},{4,5},{5,6},{6,7},{7,8},{8,9},{9,10},{10,1... | collective-permute-start | bytes 294920 | tf_op jit(solution)/shard_map/ppermute | solution.py:31
  63.7 2.2 %collective-permute-start.3 = (bf16[3,16,1024]{2,1,0:T(8,128)(2,1)S(1)}, bf16[3,16,1024]{2,1,0:T(8,128)(2,1)S(1)}, u32[]{:S(2)}, u32[]{:S(2)}) collective-permute-start(bf16[3,16,1024]{2,1,0:T(8,128)(2,1)S(1)} %get-tuple-element.40), channel_id=1, source_target_pairs={{1,0},{2,1},{3,2},{4,3},{5,4},{6,5},{7,6},{8,7},{9,8},{10,9},{11,1... | collective-permute-start | bytes 294920 | tf_op jit(solution)/shard_map/ppermute | solution.py:31
  65.9 0.0 collective-permute-done.2
  65.9 5.2 %collective-permute-done.3 = bf16[3,16,1024]{2,1,0:T(8,128)(2,1)S(1)} collective-permute-done((bf16[3,16,1024]{2,1,0:T(8,128)(2,1)S(1)}, bf16[3,16,1024]{2,1,0:T(8,128)(2,1)S(1)}, u32[]{:S(2)}, u32[]{:S(2)}) %collective-permute-start.3) | collective-permute-done | bytes 98336 | tf_op jit(solution)/shard_map/ppermute | solution.py:31
  71.2 0.5 fusion
  71.7 0.7 copy.105
  72.4 75.1 %all_to_all.19 = bf16[3,64,2048]{2,0,1:T(4,128)(2,1)S(1)} all-to-all(bf16[3,64,2048]{2,0,1:T(4,128)(2,1)S(1)} %copy.105), channel_id=1, replica_groups=mesh['space'=32,'tm'=16] {'space'}, dimensions={1} | all-to-all | bytes 1572864 | tf_op jit(solution)/shard_map/all_to_all | solution.py:155
  147.5 1.5 copy.106
  (19 shorter events, 0.3 us)
Async XLA Ops:
  0.0 9.9 %copy-start = (s32[16,2]{0,1:T(2,128)S(1)}, s32[16,2]{0,1:T(2,128)}, u32[]{:S(2)}) copy-start(s32[16,2]{0,1:T(2,128)} %param.10) | copy-start | bytes 388
  1.1 16.8 %collective-permute-start = (bf16[2,3,16,1024]{3,2,1,0:T(8,128)(2,1)S(1)}, bf16[2,3,16,1024]{3,2,1,0:T(8,128)(2,1)S(1)}, u32[]{:S(2)}, u32[]{:S(2)}) collective-permute-start(bf16[2,3,16,1024]{3,2,1,0:T(8,128)(2,1)S(1)} %get-tuple-element.42), channel_id=1, source_target_pairs={{0,1},{1,2},{2,3},{3,4},{4,5},{5,6},{6,7},{7,8},{8,9},{9,10},{10,1... | collective-permute-start | bytes 589832 | tf_op jit(solution)/shard_map/ppermute | solution.py:20
  3.9 14.0 %collective-permute-start.1 = (bf16[2,3,16,1024]{3,2,1,0:T(8,128)(2,1)S(1)}, bf16[2,3,16,1024]{3,2,1,0:T(8,128)(2,1)S(1)}, u32[]{:S(2)}, u32[]{:S(2)}) collective-permute-start(bf16[2,3,16,1024]{3,2,1,0:T(8,128)(2,1)S(1)} %get-tuple-element.43), channel_id=1, source_target_pairs={{1,0},{2,1},{3,2},{4,3},{5,4},{6,5},{7,6},{8,7},{9,8},{10,9},{11,1... | collective-permute-start | bytes 589832 | tf_op jit(solution)/shard_map/ppermute | solution.py:23
  22.5 35.7 %copy-start.1 = (s32[16,1]{0,1:T(1,128)S(1)}, s32[16,1]{0,1:T(1,128)}, u32[]{:S(2)}) copy-start(s32[16,1]{0,1:T(1,128)} %param.9) | copy-start | bytes 196
  22.5 12.4 %all-to-all-start = ((bf16[2,3,16,1536]{3,0,1,2:T(2,128)(2,1)}), bf16[2,3,16,1536]{3,0,1,2:T(2,128)(2,1)S(1)}, u32[]{:S(2)}, u32[]{:S(2)}) async-start(bf16[2,3,16,1536]{3,0,1,2:T(2,128)(2,1)} %copy.91), calls=%async_computation | async-start | bytes 589824 | tf_op jit(solution)/shard_map/all_to_all | solution.py:120
  46.0 12.5 %all-to-all-start.1 = ((bf16[16,3,1,1536]{3,1,2,0:T(4,128)(2,1)}), bf16[16,3,1,1536]{3,1,2,0:T(4,128)(2,1)S(1)}, u32[]{:S(2)}, u32[]{:S(2)}) async-start(bf16[16,3,1,1536]{3,1,2,0:T(4,128)(2,1)} %constant_dynamic-update-slice_fusion), calls=%async_computation.1 | async-start | bytes 393216 | tf_op jit(solution)/shard_map/all_to_all | solution.py:126
  60.6 5.4 %collective-permute-start.2 = (bf16[3,16,1024]{2,1,0:T(8,128)(2,1)S(1)}, bf16[3,16,1024]{2,1,0:T(8,128)(2,1)S(1)}, u32[]{:S(2)}, u32[]{:S(2)}) collective-permute-start(bf16[3,16,1024]{2,1,0:T(8,128)(2,1)S(1)} %get-tuple-element.41), channel_id=1, source_target_pairs={{0,1},{1,2},{2,3},{3,4},{4,5},{5,6},{6,7},{7,8},{8,9},{9,10},{10,1... | collective-permute-start | bytes 294920 | tf_op jit(solution)/shard_map/ppermute | solution.py:31
  63.7 7.5 %collective-permute-start.3 = (bf16[3,16,1024]{2,1,0:T(8,128)(2,1)S(1)}, bf16[3,16,1024]{2,1,0:T(8,128)(2,1)S(1)}, u32[]{:S(2)}, u32[]{:S(2)}) collective-permute-start(bf16[3,16,1024]{2,1,0:T(8,128)(2,1)S(1)} %get-tuple-element.40), channel_id=1, source_target_pairs={{1,0},{2,1},{3,2},{4,3},{5,4},{6,5},{7,6},{8,7},{9,8},{10,9},{11,1... | collective-permute-start | bytes 294920 | tf_op jit(solution)/shard_map/ppermute | solution.py:31
